TPU v7x, 32 devices: a whole 2x2x4 slice. The times are simulated.
32 devices in a mesh: blk: 8 (over z, core), head: 4 (over y, x).
Axes of the slice: x: 2, y: 2, z: 4, core: 2. Of those that a mesh axis runs over, the one named last changes fastest.
Arguments:
- queries: bfloat16 [2048, 8192], P('blk', 'head'), may hold values from -4 to 10
- context_keys: bfloat16 [8192, 1024], P('blk', 'head'), may hold values from -4 to 7
- context_values: bfloat16 [8192, 1024], P('blk', 'head'), may hold values from -6 to 6
- response_keys: bfloat16 [2048, 1024], P('blk', 'head'), may hold values from -4 to 7
- response_values: bfloat16 [2048, 1024], P('blk', 'head'), may hold values from -6 to 6
- out_weight: bfloat16 [8192, 8192], P('head', 'blk'), may hold values from -0.09375 to 0.09375
- query_docs: int32 [16], replicated, may hold values from 0 to 2
- block_docs: int32 [64], replicated, may hold values from 0 to 2
- visits: int32 [16, 4, 8], replicated, may hold values 0 or 1
Outputs:
- mixed: bfloat16 [2048, 8192], P('blk', 'head')
All inputs are finite; a program needn't handle non-finite values.
Results may differ from a plain program's by a relative error of at most 0.0165.
Values may be sent and summed in bfloat16 or wider, within the bound.
A program may use at most 128 MiB of HBM per device.

v0:
```python
import functools

import jax
import jax.numpy as jnp
from jax import lax
from jax.experimental import pallas as pl
from jax.experimental.pallas import tpu as pltpu
from jax.sharding import PartitionSpec as P

HD = 128
BLOCK = 128
HOPS = 3
PIECES = 4
HALVES = 2
MESH = pl.DeviceIdType.MESH
VMEM_BYTES = 56 * 1024 * 1024
LOG2E = 1.4426950408889634


def collect(devices, k_ref, v_ref, k_all, v_all, own_sem, send_sem, recv_sem):
    me, row = lax.axis_index("blk"), lax.axis_index("head")
    left, right = lax.rem(me + devices - 1, devices), lax.rem(me + 1, devices)
    barrier = pltpu.get_barrier_semaphore()
    for other in (left, right):
        pl.semaphore_signal(barrier, inc=1, device_id=(other, row), device_id_type=MESH)
    pl.semaphore_wait(barrier, 2)
    size = k_ref.shape[0] // PIECES

    def hop(step, which, piece):
        source, store = ((k_ref, k_all), (v_ref, v_all))[which]
        rows = pl.ds(piece * size, size)
        return pltpu.make_async_remote_copy(
            src_ref=source.at[rows] if step == 0 else store.at[step, rows],
            dst_ref=store.at[step + 1, rows],
            send_sem=send_sem.at[step, which, piece],
            recv_sem=recv_sem.at[step, which, piece],
            device_id=(left, row),
            device_id_type=MESH,
        )

    parts = [(which, piece) for piece in range(PIECES) for which in range(2)]
    for part in parts:
        hop(0, *part).start()
    own = [
        pltpu.make_async_copy(k_ref, k_all.at[0], own_sem.at[0]),
        pltpu.make_async_copy(v_ref, v_all.at[0], own_sem.at[1]),
    ]
    for copy in own:
        copy.start()
    for step in range(1, HOPS):
        for part in parts:
            hop(step - 1, *part).wait_recv()
            hop(step, *part).start()
    for part in parts:
        hop(HOPS - 1, *part).wait_recv()
    for step in range(HOPS):
        for part in parts:
            hop(step, *part).wait_send()
    for copy in own:
        copy.wait()


def attend(
    devices, kvb, qdoc_ref, bdoc_ref, visit_ref, q_ref, k_ref, v_ref, rk_ref, rv_ref, o_ref,
    chosen, turned, top, total, acc
):
    me = lax.axis_index("blk")
    block_here = pl.program_id(1)
    row_blocks = pl.num_programs(1)
    query_block = me * row_blocks + block_here
    doc = qdoc_ref[query_block]
    slots = (HOPS + 1) * kvb

    def choose(slot, count):
        step = lax.div(slot, kvb)
        holder = lax.rem(me + step, devices)
        seen = visit_ref[query_block * slots + slot] == 1
        same = bdoc_ref[holder * kvb + lax.rem(slot, kvb)] == doc
        chosen[count] = slot
        return count + jnp.where(seen & same, 1, 0)

    chosen[0] = 0
    count = lax.fori_loop(0, slots, choose, 0)
    group = q_ref.shape[1] // HD
    for j in range(group):
        turned[:, j * BLOCK : (j + 1) * BLOCK] = q_ref[:, j * HD : (j + 1) * HD].T
    scale = HD**-0.5 * LOG2E

    def scored(keys):
        return jnp.dot(keys, turned[...], preferred_element_type=jnp.float32) * scale

    def weighted(values, weights):
        return lax.dot_general(
            values,
            weights.astype(jnp.bfloat16),
            (((0,), (0,)), ((), ())),
            preferred_element_type=jnp.float32,
        )

    scores = scored(rk_ref[...])
    place = lax.rem(lax.broadcasted_iota(jnp.int32, scores.shape, 1), BLOCK) + block_here * BLOCK
    scores = jnp.where(lax.broadcasted_iota(jnp.int32, scores.shape, 0) <= place, scores, -jnp.inf)
    first = jnp.max(scores, axis=0, keepdims=True)
    weights = jnp.exp2(scores - first)
    top[...] = first
    total[...] = jnp.sum(weights, axis=0, keepdims=True)
    acc[...] = weighted(rv_ref[...], weights)

    def add(keys, values):
        scores = scored(keys)
        before = top[...]
        now = jnp.maximum(before, jnp.max(scores, axis=0, keepdims=True))
        weights = jnp.exp2(scores - now)
        factor = jnp.exp2(before - now)
        top[...] = now
        total[...] = total[...] * factor + jnp.sum(weights, axis=0, keepdims=True)
        acc[...] = acc[...] * factor + weighted(values, weights)

    def rows_of(i):
        return pl.ds(pl.multiple_of(chosen[i] * BLOCK, BLOCK), BLOCK)

    def pair(i, carry):
        one, two = rows_of(2 * i), rows_of(2 * i + 1)
        add(
            jnp.concatenate([k_ref[one, :], k_ref[two, :]], axis=0),
            jnp.concatenate([v_ref[one, :], v_ref[two, :]], axis=0),
        )
        return carry

    lax.fori_loop(0, lax.div(count, 2), pair, 0)

    @pl.when(lax.rem(count, 2) == 1)
    def _():
        last = rows_of(count - 1)
        add(k_ref[last, :], v_ref[last, :])

    result = (acc[...] / total[...]).astype(jnp.bfloat16)
    for j in range(group):
        o_ref[:, j * HD : (j + 1) * HD] = result[:, j * BLOCK : (j + 1) * BLOCK].T


def project(
    members, a_ref, w_ref, out_ref, w_pair, blocks, parts, inbox, sums,
    w_sem, a_down, a_up, a_recv, part_send, part_recv, sum_send, sum_recv
):
    me, head = lax.axis_index("blk"), lax.axis_index("head")
    spot, core = lax.div(me, 2), lax.rem(me, 2)
    half_rows = a_ref.shape[0] // HALVES
    piece = half_rows // members
    width = w_ref.shape[1]

    barrier = pltpu.get_barrier_semaphore()
    for p in range(members):
        for h in range(members):
            @pl.when((p != spot) | (h != head))
            def _():
                pl.semaphore_signal(
                    barrier, inc=1, device_id=(2 * p + core, h), device_id_type=MESH
                )
    pl.semaphore_signal(barrier, inc=1, device_id=(2 * spot + 1 - core, head), device_id_type=MESH)
    pl.semaphore_wait(barrier, members * members)

    def along(source, half, down):
        rows = pl.ds(half * half_rows, half_rows)
        return functools.partial(
            pltpu.make_async_remote_copy,
            dst_ref=blocks.at[source, rows],
            send_sem=(a_down if down else a_up).at[source, half],
            recv_sem=a_recv.at[source, half],
            device_id=(2 * (spot - 1 if down else spot + 1) + core, head),
            device_id_type=MESH,
        )

    def pass_on(source, half, own, down, act):
        rows = pl.ds(half * half_rows, half_rows)
        origin = a_ref.at[rows] if own else blocks.at[source, rows]

        @pl.when(spot > 0 if down else spot < members - 1)
        def _():
            act(along(source, half, down)(src_ref=origin))

    start = lambda copy: copy.start()
    finish = lambda copy: copy.wait_send()
    for half in range(HALVES):
        pass_on(spot, half, True, True, start)
        pass_on(spot, half, True, False, start)
    swap = pltpu.make_async_remote_copy(
        src_ref=w_ref,
        dst_ref=w_pair,
        send_sem=w_sem.at[0],
        recv_sem=w_sem.at[1],
        device_id=(2 * spot + 1 - core, head),
        device_id_type=MESH,
    )
    swap.start()

    def part_copy(source, half, k):
        peer = lax.rem(head + k, members)
        return pltpu.make_async_remote_copy(
            src_ref=parts.at[source, half, pl.ds(pl.multiple_of(peer * piece, piece), piece)],
            dst_ref=inbox.at[source, half, k - 1],
            send_sem=part_send.at[source, half, k - 1],
            recv_sem=part_recv.at[source, half, k - 1],
            device_id=(me, peer),
            device_id_type=MESH,
        )

    def sum_copy(source, half):
        rows = pl.ds(pl.multiple_of(half * half_rows + head * piece, piece), piece)
        return pltpu.make_async_remote_copy(
            src_ref=sums.at[source, half],
            dst_ref=out_ref.at[rows],
            send_sem=sum_send.at[source, half],
            recv_sem=sum_recv.at[half, head],
            device_id=(2 * source + core, spot),
            device_id_type=MESH,
        )

    def multiply(source, half, own):
        rows = pl.ds(half * half_rows, half_rows)
        left = a_ref.at[rows] if own else blocks.at[source, rows]
        tile = min(width, 512)
        for right, place in ((w_ref, core), (w_pair, 1 - core)):
            if own and half == 0 and right is w_pair:
                swap.wait_recv()

            @pl.loop(0, width // tile)
            def _(t):
                at = pl.multiple_of(t * tile, tile)
                to = pl.multiple_of(place * width + t * tile, tile)
                parts[source, half, :, pl.ds(to, tile)] = jnp.dot(
                    left[...], right[:, pl.ds(at, tile)], preferred_element_type=jnp.float32
                ).astype(jnp.bfloat16)

    def spread(source, half, own, from_above):
        if not own:
            along(source, half, from_above)(src_ref=blocks.at[source, pl.ds(half * half_rows, half_rows)]).wait_recv()
            pass_on(source, half, False, from_above, start)
        multiply(source, half, own)
        for k in range(1, members):
            part_copy(source, half, k).start()

    def reduce(source, half):
        mine = pl.ds(pl.multiple_of(head * piece, piece), piece)
        value = parts[source, half, mine, :].astype(jnp.float32)
        for k in range(1, members):
            part_copy(source, half, k).wait_recv()
            value += inbox[source, half, k - 1].astype(jnp.float32)
        here = (source == spot) & (head == spot)
        rows = pl.ds(pl.multiple_of(half * half_rows + head * piece, piece), piece)

        @pl.when(here)
        def _():
            out_ref[rows, :] = value.astype(jnp.bfloat16)

        @pl.when(jnp.logical_not(here))
        def _():
            sums[source, half] = value.astype(jnp.bfloat16)
            sum_copy(source, half).start()

    events = [(spot, half, True, False, None) for half in range(HALVES)]
    for step in range(1, members):
        for half in range(HALVES):
            events.append((spot + step, half, False, True, spot + step < members))
            events.append((spot - step, half, False, False, spot - step >= 0))

    def run(valid, work):
        if valid is None:
            work()
        else:
            pl.when(valid)(work)

    lag = 2
    for i in range(len(events) + lag):
        if i < len(events):
            source, half, own, from_above, valid = events[i]
            run(valid, functools.partial(spread, source, half, own, from_above))
        if i >= lag:
            source, half, _, _, valid = events[i - lag]
            run(valid, functools.partial(reduce, source, half))

    for source, half, own, from_above, valid in events:
        def done(source=source, half=half, own=own, from_above=from_above):
            if own:
                pass_on(source, half, True, True, finish)
                pass_on(source, half, True, False, finish)
            else:
                pass_on(source, half, False, from_above, finish)
            for k in range(1, members):
                part_copy(source, half, k).wait_send()

            @pl.when((source != spot) | (head != spot))
            def _():
                sum_copy(source, half).wait_send()

        run(valid, done)
    swap.wait_send()
    for half in range(HALVES):
        for k in range(members):
            rows = pl.ds(half * half_rows + k * piece, piece)

            @pl.when((k != head) | (spot != head))
            def _():
                pltpu.make_async_remote_copy(
                    src_ref=sums.at[0, 0],
                    dst_ref=out_ref.at[rows],
                    send_sem=sum_send.at[0, 0],
                    recv_sem=sum_recv.at[half, k],
                    device_id=(2 * head + core, k),
                    device_id_type=MESH,
                ).wait_recv()


def shards(
    queries,
    context_keys,
    context_values,
    response_keys,
    response_values,
    out_weight,
    query_docs,
    block_docs,
    visits,
):
    devices, members = lax.axis_size("blk"), lax.axis_size("head")
    assert devices == 2 * members
    rows_here, lanes = queries.shape
    key_rows, key_lanes = context_keys.shape
    heads_here = key_lanes // HD
    group = lanes // heads_here
    kvb = key_rows // BLOCK
    slots = HOPS + 1
    dma = pltpu.SemaphoreType.DMA
    anywhere = pl.BlockSpec(memory_space=pl.ANY)
    in_vmem = pl.BlockSpec(memory_space=pltpu.VMEM)
    in_smem = pl.BlockSpec(memory_space=pltpu.SMEM)

    store = jax.ShapeDtypeStruct((slots, key_rows, key_lanes), jnp.bfloat16)
    all_keys, all_values = pl.pallas_call(
        functools.partial(collect, devices),
        out_shape=(store, store),
        in_specs=[anywhere] * 2,
        out_specs=(anywhere, anywhere),
        scratch_shapes=[dma((2,)), dma((HOPS, 2, PIECES)), dma((HOPS, 2, PIECES))],
        compiler_params=pltpu.CompilerParams(
            collective_id=0, has_side_effects=True, vmem_limit_bytes=VMEM_BYTES
        ),
        name="collect",
    )(context_keys, context_values)

    whole = lambda: pl.BlockSpec((slots * key_rows, HD), lambda g, b: (0, g))
    own = lambda: pl.BlockSpec((rows_here, HD), lambda g, b: (0, g))
    attended = pl.pallas_call(
        functools.partial(attend, devices, kvb),
        grid=(heads_here, rows_here // BLOCK),
        out_shape=jax.ShapeDtypeStruct((rows_here, lanes), jnp.bfloat16),
        in_specs=[in_smem] * 3
        + [pl.BlockSpec((BLOCK, group), lambda g, b: (b, g)), whole(), whole(), own(), own()],
        out_specs=pl.BlockSpec((BLOCK, group), lambda g, b: (b, g)),
        scratch_shapes=[
            pltpu.SMEM((slots * kvb + 1,), jnp.int32),
            pltpu.VMEM((HD, group // HD * BLOCK), jnp.bfloat16),
            pltpu.VMEM((1, group // HD * BLOCK), jnp.float32),
            pltpu.VMEM((1, group // HD * BLOCK), jnp.float32),
            pltpu.VMEM((HD, group // HD * BLOCK), jnp.float32),
        ],
        compiler_params=pltpu.CompilerParams(vmem_limit_bytes=VMEM_BYTES),
        name="attend",
    )(
        query_docs,
        block_docs,
        visits.reshape(-1),
        queries,
        all_keys.reshape(slots * key_rows, key_lanes),
        all_values.reshape(slots * key_rows, key_lanes),
        response_keys,
        response_values,
    )

    depth, width = out_weight.shape
    half_rows = rows_here // HALVES
    piece = half_rows // members
    half = jnp.bfloat16
    return pl.pallas_call(
        functools.partial(project, members),
        out_shape=jax.ShapeDtypeStruct((rows_here, 2 * width), half),
        in_specs=[in_vmem] * 2,
        out_specs=in_vmem,
        scratch_shapes=[
            pltpu.VMEM((depth, width), half),
            pltpu.VMEM((members, rows_here, depth), half),
            pltpu.VMEM((members, HALVES, half_rows, 2 * width), half),
            pltpu.VMEM((members, HALVES, members - 1, piece, 2 * width), half),
            pltpu.VMEM((members, HALVES, piece, 2 * width), half),
            dma((2,)),
            dma((members, HALVES)),
            dma((members, HALVES)),
            dma((members, HALVES)),
            dma((members, HALVES, members - 1)),
            dma((members, HALVES, members - 1)),
            dma((members, HALVES)),
            dma((HALVES, members)),
        ],
        compiler_params=pltpu.CompilerParams(
            collective_id=1, has_side_effects=True, vmem_limit_bytes=VMEM_BYTES
        ),
        name="project",
    )(attended, out_weight)


def solution(mesh):
    in_specs = (
        P("blk", "head"),
        P("blk", "head"),
        P("blk", "head"),
        P("blk", "head"),
        P("blk", "head"),
        P("head", "blk"),
        P(),
        P(),
        P(),
    )
    out_specs = P("blk", "head")
    return jax.shard_map(shards, mesh=mesh, in_specs=in_specs, out_specs=out_specs, check_vma=False)
```

profile of v0, /device:TPU:6, one launch (start us, length us, event | category | flops | bytes accessed | tf_op | source)
XLA Modules:
  0.0 168.4 jit_solution(12053035067358548657)
XLA Ops:
  0.0 0.8 copy.10
  0.8 0.7 reshape.9.visit_ref
  1.5 38.6 %collect.1 = (bf16[4,1024,256]{2,1,0:T(8,128)(2,1)}, bf16[4,1024,256]{2,1,0:T(8,128)(2,1)}) custom-call(bf16[1024,256]{1,0:T(8,128)(2,1)} %k_ref.1, bf16[1024,256]{1,0:T(8,128)(2,1)} %v_ref.1), custom_call_target="tpu_custom_call" | custom-call | tf_op jit(solution)/shard_map/collect/pallas_call | solution.py:339
  40.1 19.0 %attend.1.a_ref = bf16[256,2048]{1,0:T(8,128)(2,1)} custom-call(s32[16]{0:T(128)} %qdoc_ref.1, s32[64]{0:T(128)} %bdoc_ref.1, s32[512]{0:T(512)} %reshape.9.visit_ref, bf16[256,2048]{1,0:T(8,128)(2,1)} %q_ref.1, bf16[4096,256]{1,0:T(8,128)(2,1)} %bitcast.2, bf16[4096,256]{1,0:T(8,128)(2,1)} %bitcast.3, bf16[256,256]{1,0:T(8,128)(2,1)} %rk_ref.1, ...), custom_call_target="tpu_custom_call" | custom-call | tf_op jit(solution)/shard_map/attend/pallas_call | solution.py:353
  59.1 107.0 %project.1 = bf16[256,2048]{1,0:T(8,128)(2,1)} custom-call(bf16[256,2048]{1,0:T(8,128)(2,1)} %attend.1.a_ref, bf16[2048,1024]{1,0:T(8,128)(2,1)} %w_ref.1), custom_call_target="tpu_custom_call" | custom-call | tf_op jit(solution)/shard_map/project/pallas_call | solution.py:384
  166.1 2.3 %copy.12 = bf16[256,2048]{1,0:T(8,128)(2,1)} copy(bf16[256,2048]{1,0:T(8,128)(2,1)} %project.1) | data formatting | bytes 2097152
where the time goes:
time: 171 us; the launch traced here: 168 us
  Pallas kernels  165 us (96%)
  local copies, waits for them, and re-layouts  3.78 us (2%)
    pallas_call x1, Pallas kernels, shards(): pl.pallas_call(functools.partial(project, members), out_shape=jax.ShapeDt...  107 us
    pallas_call x1, Pallas kernels, shards(): pl.pallas_call(functools.partial(collect, devices), out_shape=(store, sto...  38.6 us
    pallas_call x1, Pallas kernels, shards(): pl.pallas_call(functools.partial(attend, devices, kvb), grid=(heads_here,...  19 us

commit v1 on v0

--- a/solution.py
+++ b/solution.py
@@ -11,7 +11,7 @@
 BLOCK = 128
 HOPS = 3
 PIECES = 4
-HALVES = 2
+MIN_ROWS = 16
 MESH = pl.DeviceIdType.MESH
 VMEM_BYTES = 56 * 1024 * 1024
 LOG2E = 1.4426950408889634
@@ -140,14 +140,16 @@
 
 
 def project(
-    members, a_ref, w_ref, out_ref, w_pair, blocks, parts, inbox, sums,
+    members, a_ref, w_ref, out_ref, w_own, w_pair, blocks, parts, inbox, sums,
     w_sem, a_down, a_up, a_recv, part_send, part_recv, sum_send, sum_recv
 ):
     me, head = lax.axis_index("blk"), lax.axis_index("head")
     spot, core = lax.div(me, 2), lax.rem(me, 2)
-    half_rows = a_ref.shape[0] // HALVES
-    piece = half_rows // members
+    chunks, piece = sums.shape[1:3]
+    half_rows = piece * members
     width = w_ref.shape[1]
+    load = pltpu.make_async_copy(w_ref, w_own, w_sem.at[2])
+    load.start()
 
     barrier = pltpu.get_barrier_semaphore()
     for p in range(members):
@@ -181,7 +183,7 @@
 
     start = lambda copy: copy.start()
     finish = lambda copy: copy.wait_send()
-    for half in range(HALVES):
+    for half in range(chunks):
         pass_on(spot, half, True, True, start)
         pass_on(spot, half, True, False, start)
     swap = pltpu.make_async_remote_copy(
@@ -220,9 +222,12 @@
         rows = pl.ds(half * half_rows, half_rows)
         left = a_ref.at[rows] if own else blocks.at[source, rows]
         tile = min(width, 512)
-        for right, place in ((w_ref, core), (w_pair, 1 - core)):
-            if own and half == 0 and right is w_pair:
-                swap.wait_recv()
+        for right, place in ((w_own, core), (w_pair, 1 - core)):
+            if own and half == 0:
+                if right is w_pair:
+                    swap.wait_recv()
+                else:
+                    load.wait()
 
             @pl.loop(0, width // tile)
             def _(t):
@@ -258,9 +263,9 @@
             sums[source, half] = value.astype(jnp.bfloat16)
             sum_copy(source, half).start()
 
-    events = [(spot, half, True, False, None) for half in range(HALVES)]
+    events = [(spot, half, True, False, None) for half in range(chunks)]
     for step in range(1, members):
-        for half in range(HALVES):
+        for half in range(chunks):
             events.append((spot + step, half, False, True, spot + step < members))
             events.append((spot - step, half, False, False, spot - step >= 0))
 
@@ -295,7 +300,7 @@
 
         run(valid, done)
     swap.wait_send()
-    for half in range(HALVES):
+    for half in range(chunks):
         for k in range(members):
             rows = pl.ds(half * half_rows + k * piece, piece)
 
@@ -378,28 +383,30 @@
     )
 
     depth, width = out_weight.shape
-    half_rows = rows_here // HALVES
+    chunks = rows_here // (MIN_ROWS * members)
+    half_rows = rows_here // chunks
     piece = half_rows // members
     half = jnp.bfloat16
     return pl.pallas_call(
         functools.partial(project, members),
         out_shape=jax.ShapeDtypeStruct((rows_here, 2 * width), half),
-        in_specs=[in_vmem] * 2,
+        in_specs=[in_vmem, anywhere],
         out_specs=in_vmem,
         scratch_shapes=[
             pltpu.VMEM((depth, width), half),
+            pltpu.VMEM((depth, width), half),
             pltpu.VMEM((members, rows_here, depth), half),
-            pltpu.VMEM((members, HALVES, half_rows, 2 * width), half),
-            pltpu.VMEM((members, HALVES, members - 1, piece, 2 * width), half),
-            pltpu.VMEM((members, HALVES, piece, 2 * width), half),
-            dma((2,)),
-            dma((members, HALVES)),
-            dma((members, HALVES)),
-            dma((members, HALVES)),
-            dma((members, HALVES, members - 1)),
-            dma((members, HALVES, members - 1)),
-            dma((members, HALVES)),
-            dma((HALVES, members)),
+            pltpu.VMEM((members, chunks, half_rows, 2 * width), half),
+            pltpu.VMEM((members, chunks, members - 1, piece, 2 * width), half),
+            pltpu.VMEM((members, chunks, piece, 2 * width), half),
+            dma((3,)),
+            dma((members, chunks)),
+            dma((members, chunks)),
+            dma((members, chunks)),
+            dma((members, chunks, members - 1)),
+            dma((members, chunks, members - 1)),
+            dma((members, chunks)),
+            dma((chunks, members)),
         ],
         compiler_params=pltpu.CompilerParams(
             collective_id=1, has_side_effects=True, vmem_limit_bytes=VMEM_BYTES

time: 171 us -> 170 us (level)
    pallas_call x1, Pallas kernels: 107 us -> 112 us  [shards(): pl.pallas_call(functools.partial(project, members), out_shape=jax.ShapeDt...]
    pallas_call x1, Pallas kernels: 19 us -> 14.7 us  [shards(): pl.pallas_call(functools.partial(attend, devices, kvb), grid=(heads_here,...]
where the time goes in v1:
time: 170 us; the launch traced here: 169 us
  Pallas kernels  165 us (97%)
  local copies, waits for them, and re-layouts  3.78 us (2%)
    pallas_call x1, Pallas kernels, shards(): pl.pallas_call(functools.partial(project, members), out_shape=jax.ShapeDt...  112 us
    pallas_call x1, Pallas kernels, shards(): pl.pallas_call(functools.partial(collect, devices), out_shape=(store, sto...  38.6 us
    pallas_call x1, Pallas kernels, shards(): pl.pallas_call(functools.partial(attend, devices, kvb), grid=(heads_here,...  14.7 us

profile of v1, /device:TPU:6, one launch (start us, length us, event | category | flops | bytes accessed | tf_op | source)
XLA Modules:
  0.0 168.8 jit_solution(11620934185776798237)
XLA Ops:
  0.0 0.8 copy.10
  0.8 0.7 reshape.9.visit_ref
  1.5 38.6 %collect.1 = (bf16[4,1024,256]{2,1,0:T(8,128)(2,1)}, bf16[4,1024,256]{2,1,0:T(8,128)(2,1)}) custom-call(bf16[1024,256]{1,0:T(8,128)(2,1)} %k_ref.1, bf16[1024,256]{1,0:T(8,128)(2,1)} %v_ref.1), custom_call_target="tpu_custom_call" | custom-call | tf_op jit(solution)/shard_map/collect/pallas_call | solution.py:344
  40.1 14.7 %attend.1.a_ref = bf16[256,2048]{1,0:T(8,128)(2,1)} custom-call(s32[16]{0:T(128)} %qdoc_ref.1, s32[64]{0:T(128)} %bdoc_ref.1, s32[512]{0:T(512)} %reshape.9.visit_ref, bf16[256,2048]{1,0:T(8,128)(2,1)} %q_ref.1, bf16[4096,256]{1,0:T(8,128)(2,1)} %bitcast.2, bf16[4096,256]{1,0:T(8,128)(2,1)} %bitcast.3, bf16[256,256]{1,0:T(8,128)(2,1)} %rk_ref.1, ...), custom_call_target="tpu_custom_call" | custom-call | tf_op jit(solution)/shard_map/attend/pallas_call | solution.py:358
  54.8 111.6 %project.1 = bf16[256,2048]{1,0:T(8,128)(2,1)} custom-call(bf16[256,2048]{1,0:T(8,128)(2,1)} %attend.1.a_ref, bf16[2048,1024]{1,0:T(8,128)(2,1)} %w_ref.1), custom_call_target="tpu_custom_call" | custom-call | tf_op jit(solution)/shard_map/project/pallas_call | solution.py:390
  166.5 2.3 %copy.12 = bf16[256,2048]{1,0:T(8,128)(2,1)} copy(bf16[256,2048]{1,0:T(8,128)(2,1)} %project.1) | data formatting | bytes 2097152
